TPU v7x, 32 devices: a whole 2x2x4 slice. The times are simulated.
32 devices in a mesh: lev: 2 (over x), tile: 16 (over z, y, core).
Axes of the slice: x: 2, y: 2, z: 4, core: 2. Of those that a mesh axis runs over, the one named last changes fastest.
Arguments:
- adjoint: float32 [5, 16, 256, 256], P(None, 'lev', 'tile'), may hold values from -6 to 6
- courant: float32 [2, 16, 256, 256], P(None, 'lev', 'tile'), may hold values from -0.6 to 0.6
- metric: float32 [2, 16, 256, 256], P(None, 'lev', 'tile'), may hold values from 0.5 to 2
- pivot_inverse: float32 [4, 16, 256, 256], P(None, 'lev', 'tile'), may hold values from -0.06 to 0.2
- lower_gain: float32 [4, 16, 256, 256], P(None, 'lev', 'tile'), may hold values from -0.5 to 1
- upper_gain: float32 [4, 16, 256, 256], P(None, 'lev', 'tile'), may hold values from -0.5 to 1
Outputs:
- stepped: float32 [5, 16, 256, 256], P(None, 'lev', 'tile')
All inputs are finite; a program needn't handle non-finite values.
Results may differ from a plain program's by a relative error of at most 0.00002.
Values sent between devices are 32-bit elements; how exact they have to be, the bound alone decides.
No kernel may reach another device: no remote copies, remote signals or barrier semaphores. Data moves between devices by JAX's collectives and lax.ppermute only.
A program may use at most 64 MiB of HBM per device.

v0:
```python
import jax
import jax.numpy as jnp
from jax import lax
from jax.experimental import pallas as pl
from jax.experimental.pallas import tpu as pltpu
from jax.sharding import PartitionSpec as P

F32 = jnp.float32
VMEM_LIMIT = 24 * 1024 * 1024


def held(shape):
    return pltpu.VMEM(shape, F32)


def whole():
    return pl.BlockSpec(memory_space=pltpu.VMEM)


def params():
    return pltpu.CompilerParams(vmem_limit_bytes=VMEM_LIMIT)


def mul(m, v):
    return (m[0] * v[0] + m[1] * v[1], m[2] * v[0] + m[3] * v[1])


def matmul(m, n):
    return (
        m[0] * n[0] + m[1] * n[2],
        m[0] * n[1] + m[1] * n[3],
        m[2] * n[0] + m[3] * n[2],
        m[2] * n[1] + m[3] * n[3],
    )


def add(a, b):
    return tuple(x + y for x, y in zip(a, b, strict=True))


def at(ref, level):
    return tuple(ref[k, level] for k in range(ref.shape[0]))


def even_tile():
    return lax.rem(lax.axis_index("tile"), 2) == 0


def edges_body(adj, courant, metric, chip, far):
    rows = adj.shape[2]

    def emit(out, first):
        for r in range(2):
            wind = courant[0, :, first + r, :]
            for k in range(4):
                out[k, r] = wind * adj[k, :, first + r, :]
            out[4, r] = (
                wind * adj[4, :, first + r, :]
                + metric[0, :, first + r, :] * adj[0, :, first + r, :]
            )

    @pl.when(even_tile())
    def _():
        emit(chip, rows - 2)
        emit(far, 0)

    @pl.when(jnp.logical_not(even_tile()))
    def _():
        emit(chip, 0)
        emit(far, rows - 2)


def across(q):
    rows = q.shape[0]
    spot = lax.broadcasted_iota(jnp.int32, q.shape, 0)
    out = None
    for step, weight in ((1, 8.0 / 12.0), (2, -1.0 / 12.0)):
        ahead = jnp.where(spot < rows - step, pltpu.roll(q, rows - step, 0), 0.0)
        behind = jnp.where(spot >= step, pltpu.roll(q, step, 0), 0.0)
        term = weight * (ahead - behind)
        out = term if out is None else out + term
    return out


def along(q):
    cols = q.shape[1]
    near = pltpu.roll(q, cols - 1, 1) - pltpu.roll(q, 1, 1)
    wide = pltpu.roll(q, cols - 2, 1) - pltpu.roll(q, 2, 1)
    return (8.0 / 12.0) * near - (1.0 / 12.0) * wide


def inner_body(adj, courant, metric, lower, upper, passive, active, response):
    levels = adj.shape[1]

    def one(l, _):
        c0, c1 = courant[0, l], courant[1, l]
        for k, slot in ((0, 0), (1, 1), (3, 2)):
            x = adj[k, l]
            passive[slot, l] = x + across(c0 * x) + along(c1 * x)
        x = adj[2, l]
        active[0, l] = x + across(c0 * x) + along(c1 * x)
        x = adj[4, l]
        active[1, l] = (
            x
            + across(c0 * x + metric[0, l] * adj[0, l])
            + along(c1 * x + metric[1, l] * adj[1, l])
        )
        return 0

    lax.fori_loop(0, levels, one, 0)
    chain = [at(lower, 0)]
    for l in range(1, levels):
        chain.append(matmul(at(lower, l), chain[-1]))
    total = chain[-1]
    for l in range(levels - 2, -1, -1):
        total = add(matmul(at(upper, l), total), chain[l])
    for k in range(4):
        response[k] = total[k]


def halo_rows(chip, far, field):
    even = even_tile()
    got_chip = [chip[field, r] for r in range(2)]
    got_far = [far[field, r] for r in range(2)]
    low = [jnp.where(even, b, a) for a, b in zip(got_chip, got_far, strict=True)]
    high = [jnp.where(even, a, b) for a, b in zip(got_chip, got_far, strict=True)]
    return low, high


def add_halo(ref, slot, low, high):
    rows = ref.shape[2]
    near, wide = 8.0 / 12.0, 1.0 / 12.0
    ref[slot, :, 0, :] = ref[slot, :, 0, :] + (wide * low[0] - near * low[1])
    ref[slot, :, 1, :] = ref[slot, :, 1, :] + wide * low[1]
    ref[slot, :, rows - 2, :] = ref[slot, :, rows - 2, :] - wide * high[0]
    ref[slot, :, rows - 1, :] = ref[slot, :, rows - 1, :] + (
        near * high[0] - wide * high[1]
    )


def sweep_body(active, pivot, lower, upper, response, chip, far, lowered, summary, held_active):
    levels = active.shape[1]
    held_active[...] = active[...]
    for slot, field in ((0, 2), (1, 4)):
        add_halo(held_active, slot, *halo_rows(chip, far, field))
    states = []
    for l in range(levels):
        fresh = mul(at(pivot, l), at(held_active, l))
        if states:
            fresh = add(mul(at(lower, l), states[-1]), fresh)
        states.append(fresh)
        for k in range(2):
            lowered[k, l] = fresh[k]

    @pl.when(lax.axis_index("lev") == 0)
    def _():
        for k in range(2):
            summary[k] = states[-1][k]

    @pl.when(lax.axis_index("lev") == 1)
    def _():
        state = at(lowered, levels - 1)
        for l in range(levels - 2, -1, -1):
            state = add(mul(at(upper, l), state), at(lowered, l))
        for k in range(2):
            summary[k] = state[k]
        for k in range(4):
            summary[2 + k] = response[k]


def passive_body(passive, chip, far, out, held_passive, sems):
    held_passive[...] = passive[...]
    copies = []
    for slot, field in ((0, 0), (1, 1), (2, 3)):
        add_halo(held_passive, slot, *halo_rows(chip, far, field))
        copies.append(
            pltpu.make_async_copy(held_passive.at[slot], out.at[field], sems.at[slot])
        )
        copies[-1].start()
    for copy in copies:
        copy.wait()


def solve_body(lowered, lower, upper, mine, summary, partial, out, solved, sems):
    del partial
    levels = lowered.shape[1]

    @pl.when(lax.axis_index("lev") == 0)
    def _():
        state = (mine[0], mine[1])
        gain = tuple(summary[2 + k] for k in range(4))
        state = add(mul(gain, state), (summary[0], summary[1]))
        for l in range(levels - 1, -1, -1):
            state = add(mul(at(upper, l), state), at(lowered, l))
            for k in range(2):
                solved[k, l] = state[k]

    @pl.when(lax.axis_index("lev") == 1)
    def _():
        entering = (summary[0], summary[1])
        full = []
        for l in range(levels):
            entering = mul(at(lower, l), entering)
            full.append(add(entering, at(lowered, l)))
        state = full[-1]
        for l in range(levels - 1, -1, -1):
            if l < levels - 1:
                state = add(mul(at(upper, l), state), full[l])
            for k in range(2):
                solved[k, l] = state[k]

    copies = [
        pltpu.make_async_copy(solved.at[k], out.at[field], sems.at[k])
        for k, field in ((0, 2), (1, 4))
    ]
    for copy in copies:
        copy.start()
    for copy in copies:
        copy.wait()


def local_pair(adjoint, courant, metric, pivot_inverse, lower_gain, upper_gain):
    fields, levels, rows, cols = adjoint.shape
    tiles = lax.axis_size("tile")
    chip, far = pl.pallas_call(
        edges_body,
        name="edges",
        in_specs=[whole()] * 3,
        out_specs=[whole()] * 2,
        out_shape=[held((fields, 2, levels, cols))] * 2,
        compiler_params=params(),
    )(adjoint, courant, metric)
    with_chip = [(i, i ^ 1) for i in range(tiles)]
    with_far = [(i, (i - 1 if i % 2 == 0 else i + 1) % tiles) for i in range(tiles)]
    got_far = lax.ppermute(far, "tile", with_far)
    got_chip = lax.ppermute(chip, "tile", with_chip)
    passive, active, response = pl.pallas_call(
        inner_body,
        name="inner",
        in_specs=[whole()] * 5,
        out_specs=[whole()] * 3,
        out_shape=[
            held((3, levels, rows, cols)),
            held((2, levels, rows, cols)),
            held((4, rows, cols)),
        ],
        compiler_params=params(),
    )(adjoint, courant, metric, lower_gain, upper_gain)
    lowered, summary = pl.pallas_call(
        sweep_body,
        name="sweep",
        in_specs=[whole()] * 7,
        out_specs=[whole()] * 2,
        out_shape=[held((2, levels, rows, cols)), held((6, rows, cols))],
        scratch_shapes=[pltpu.VMEM((2, levels, rows, cols), F32)],
        compiler_params=params(),
    )(active, pivot_inverse, lower_gain, upper_gain, response, got_chip, got_far)
    received = lax.ppermute(summary, "lev", [(0, 1), (1, 0)])
    partial = pl.pallas_call(
        passive_body,
        name="passive",
        in_specs=[whole()] * 3,
        out_specs=pl.BlockSpec(memory_space=pl.ANY),
        out_shape=jax.ShapeDtypeStruct(adjoint.shape, F32),
        scratch_shapes=[
            pltpu.VMEM((3, levels, rows, cols), F32),
            pltpu.SemaphoreType.DMA((3,)),
        ],
        compiler_params=params(),
    )(passive, got_chip, got_far)
    return pl.pallas_call(
        solve_body,
        name="solve",
        in_specs=[whole()] * 5 + [pl.BlockSpec(memory_space=pl.ANY)],
        out_specs=pl.BlockSpec(memory_space=pl.ANY),
        out_shape=jax.ShapeDtypeStruct(adjoint.shape, F32),
        scratch_shapes=[
            pltpu.VMEM((2, levels, rows, cols), F32),
            pltpu.SemaphoreType.DMA((2,)),
        ],
        input_output_aliases={5: 0},
        compiler_params=params(),
    )(lowered, lower_gain, upper_gain, summary, received, partial)


LEVEL_UNROLL = 16


def with_halo(block, sides, width):
    for axis, dim in sides:
        count = lax.axis_size(axis)
        forward = [(i, i + 1) for i in range(count - 1)]
        forward.append((count - 1, 0))
        backward = [(target, source) for source, target in forward]
        low = lax.ppermute(
            lax.slice_in_dim(block, block.shape[dim] - width, None, axis=dim), axis, forward
        )
        high = lax.ppermute(lax.slice_in_dim(block, 0, width, axis=dim), axis, backward)
        block = jnp.concatenate([low, block, high], axis=dim)
    return block


def centered_roll(values, axis_id):
    ahead_one = jnp.roll(values, -1, axis_id)
    behind_one = jnp.roll(values, 1, axis_id)
    ahead_two = jnp.roll(values, -2, axis_id)
    behind_two = jnp.roll(values, 2, axis_id)
    return (8.0 * (ahead_one - behind_one) - (ahead_two - behind_two)) / 12.0


def centered_padded(padded):
    ahead_one = padded[:, :, 3:-1, :]
    behind_one = padded[:, :, 1:-3, :]
    ahead_two = padded[:, :, 4:, :]
    behind_two = padded[:, :, :-4, :]
    return (8.0 * (ahead_one - behind_one) - (ahead_two - behind_two)) / 12.0


def mat_vec(system_matrix, vector):
    return jnp.stack(
        [
            system_matrix[0] * vector[0] + system_matrix[1] * vector[1],
            system_matrix[2] * vector[0] + system_matrix[3] * vector[1],
        ]
    )


def chain_run(coupling, forcing, initial, backward):

    def advance(state, inputs):
        fresh = mat_vec(inputs[0], state) + inputs[1]
        return (fresh, fresh)

    final_state, states = lax.scan(
        advance,
        initial,
        (jnp.moveaxis(coupling, 1, 0), jnp.moveaxis(forcing, 1, 0)),
        reverse=backward,
        unroll=min(LEVEL_UNROLL, coupling.shape[1]),
    )
    return jnp.moveaxis(states, 0, 1)


def column_solve(pieces):
    forcing, lower_part, upper_part = pieces
    initial = jnp.zeros((2,) + forcing.shape[2:], jnp.float32)
    lowered = chain_run(lower_part, forcing, initial, False)
    solved = chain_run(upper_part, lowered, initial, True)
    return lax.all_to_all(solved, "lev", split_axis=1, concat_axis=2, tiled=True)


def local_any(adjoint, courant, metric, pivot_inverse, lower_gain, upper_gain):
    weighted = jnp.concatenate([courant[0] * adjoint, (metric[0] * adjoint[0])[None]], 0)
    padded = with_halo(weighted, (("tile", 2),), 2)
    across = centered_padded(padded)
    advected = adjoint + across[:5] + centered_roll(courant[1] * adjoint, 3)
    pressure_field = advected[4] + across[5] + centered_roll(metric[1] * adjoint[1], 2)
    forcing = mat_vec(pivot_inverse, jnp.stack([advected[2], pressure_field]))
    solved = column_solve(
        (
            lax.all_to_all(forcing, "lev", split_axis=2, concat_axis=1, tiled=True),
            lax.all_to_all(lower_gain, "lev", split_axis=2, concat_axis=1, tiled=True),
            lax.all_to_all(upper_gain, "lev", split_axis=2, concat_axis=1, tiled=True),
        )
    )
    return jnp.stack([advected[0], advected[1], solved[0], advected[3], solved[1]])


def solution(mesh):
    placed = (P(None, "lev", "tile", None),) * 6
    pair = mesh.shape["lev"] == 2 and mesh.shape["tile"] % 2 == 0
    return jax.shard_map(
        local_pair if pair else local_any,
        mesh=mesh,
        in_specs=placed,
        out_specs=P(None, "lev", "tile", None),
        check_vma=False,
    )
```

profile of v0, /device:TPU:0, one launch (start us, length us, event | category | flops | bytes accessed | tf_op | source)
XLA Modules:
  0.0 17.1 jit_solution(16699823908919987865)
XLA Ops:
  0.0 0.0 copy-start.1
  0.0 0.0 copy-start
  0.0 0.0 copy-start.2
  0.0 1.2 %copy-done.2 = f32[5,8,16,256]{3,2,1,0:T(8,128)S(1)} copy-done((f32[5,8,16,256]{3,2,1,0:T(8,128)S(1)}, f32[5,8,16,256]{3,2,1,0:T(8,128)}, u32[]{:S(2)}) %copy-start.2) | copy-done | bytes 655384
  1.2 0.0 copy-start.3
  1.2 0.9 %copy-done.3 = f32[2,8,16,256]{3,2,1,0:T(8,128)S(1)} copy-done((f32[2,8,16,256]{3,2,1,0:T(8,128)S(1)}, f32[2,8,16,256]{3,2,1,0:T(8,128)}, u32[]{:S(2)}) %copy-start.3) | copy-done | bytes 262168
  2.1 0.0 copy-start.4
  2.1 0.9 %copy-done.4 = f32[2,8,16,256]{3,2,1,0:T(8,128)S(1)} copy-done((f32[2,8,16,256]{3,2,1,0:T(8,128)S(1)}, f32[2,8,16,256]{3,2,1,0:T(8,128)}, u32[]{:S(2)}) %copy-start.4) | copy-done | bytes 262168
  3.1 0.1 edges.1
  3.2 0.5 %collective-permute-start = (f32[5,2,8,256]{3,2,1,0:T(8,128)S(1)}, f32[5,2,8,256]{3,2,1,0:T(8,128)S(1)}, u32[]{:S(2)}, u32[]{:S(2)}) collective-permute-start(f32[5,2,8,256]{3,2,1,0:T(8,128)S(1)} %get-tuple-element.14), channel_id=1, source_target_pairs={{0,1},{1,0},{2,3},{3,2},{4,5},{5,4},{6,7},{7,6},{8,9},{9,8},{10,11... | collective-permute-start | bytes 245768 | tf_op jit(solution)/shard_map/ppermute | solution.py:236
  3.7 0.0 copy-start.5
  3.7 5.7 %collective-permute-start.1 = (f32[5,2,8,256]{3,2,1,0:T(8,128)S(1)}, f32[5,2,8,256]{3,2,1,0:T(8,128)S(1)}, u32[]{:S(2)}, u32[]{:S(2)}) collective-permute-start(f32[5,2,8,256]{3,2,1,0:T(8,128)S(1)} %get-tuple-element.15), channel_id=1, source_target_pairs={{0,15},{1,2},{2,1},{3,4},{4,3},{5,6},{6,5},{7,8},{8,7},{9,10},{10,... | collective-permute-start | bytes 245768 | tf_op jit(solution)/shard_map/ppermute | solution.py:235
  9.4 0.0 copy-done.1
  9.4 0.0 copy-done
  9.4 1.4 %inner.1 = (f32[3,8,16,256]{3,2,1,0:T(8,128)S(1)}, f32[2,8,16,256]{3,2,1,0:T(8,128)S(1)}, f32[4,16,256]{2,1,0:T(8,128)S(1)}) custom-call(f32[5,8,16,256]{3,2,1,0:T(8,128)S(1)} %copy-done.2, f32[2,8,16,256]{3,2,1,0:T(8,128)S(1)} %copy-done.3, f32[2,8,16,256]{3,2,1,0:T(8,128)S(1)} %copy-done.4, f32[4,8,16,256]{3,2,1,0:T(8,128)S(1)} %copy-done, ...), custom_call_target="tpu_custom_call" | custom-call | tf_op jit(solution)/shard_map/inner/pallas_call | solution.py:237
  10.8 0.0 collective-permute-done.chip
  10.8 0.7 %collective-permute-done.1.far = f32[5,2,8,256]{3,2,1,0:T(8,128)S(1)} collective-permute-done((f32[5,2,8,256]{3,2,1,0:T(8,128)S(1)}, f32[5,2,8,256]{3,2,1,0:T(8,128)S(1)}, u32[]{:S(2)}, u32[]{:S(2)}) %collective-permute-start.1) | collective-permute-done | bytes 81952 | tf_op jit(solution)/shard_map/ppermute | solution.py:235
  11.5 0.0 copy-done.5
  11.5 0.1 sweep.1
  11.6 1.6 %collective-permute-start.2 = (f32[6,16,256]{2,1,0:T(8,128)S(1)}, f32[6,16,256]{2,1,0:T(8,128)S(1)}, u32[]{:S(2)}, u32[]{:S(2)}) collective-permute-start(f32[6,16,256]{2,1,0:T(8,128)S(1)} %get-tuple-element.17.mine), channel_id=1, source_target_pairs={{0,16},{16,0},{1,17},{17,1},{2,18},{18,2},{3,19},{19,3},{4,20},{20... | collective-permute-start | bytes 294920 | tf_op jit(solution)/shard_map/ppermute | solution.py:258
  13.2 0.8 %passive.1.partial = f32[5,8,16,256]{3,2,1,0:T(8,128)} custom-call(f32[3,8,16,256]{3,2,1,0:T(8,128)S(1)} %get-tuple-element.18.passive, f32[5,2,8,256]{3,2,1,0:T(8,128)S(1)} %collective-permute-done.chip, f32[5,2,8,256]{3,2,1,0:T(8,128)S(1)} %collective-permute-done.1.far), custom_call_target="tpu_custom_call" | custom-call | tf_op jit(solution)/shard_map/passive/pallas_call | solution.py:259
  14.1 2.3 %collective-permute-done.2.summary = f32[6,16,256]{2,1,0:T(8,128)S(1)} collective-permute-done((f32[6,16,256]{2,1,0:T(8,128)S(1)}, f32[6,16,256]{2,1,0:T(8,128)S(1)}, u32[]{:S(2)}, u32[]{:S(2)}) %collective-permute-start.2) | collective-permute-done | bytes 98336 | tf_op jit(solution)/shard_map/ppermute | solution.py:258
  16.3 0.8 %solve.1 = f32[5,8,16,256]{3,2,1,0:T(8,128)} custom-call(f32[2,8,16,256]{3,2,1,0:T(8,128)S(1)} %get-tuple-element.16.lowered, f32[4,8,16,256]{3,2,1,0:T(8,128)S(1)} %copy-done, f32[4,8,16,256]{3,2,1,0:T(8,128)S(1)} %copy-done.1, f32[6,16,256]{2,1,0:T(8,128)S(1)} %get-tuple-element.17.mine, ...), custom_call_target="tpu_custom_call", output_to_operand_aliasing={{}: (5, {})} | custom-call | tf_op jit(solution)/shard_map/solve/pallas_call | solution.py:271
Async XLA Ops:
  0.0 9.4 %copy-start.1 = (f32[4,8,16,256]{3,2,1,0:T(8,128)S(1)}, f32[4,8,16,256]{3,2,1,0:T(8,128)}, u32[]{:S(2)}) copy-start(f32[4,8,16,256]{3,2,1,0:T(8,128)} %upper.5) | copy-start | bytes 1572868
  0.0 9.4 %copy-start = (f32[4,8,16,256]{3,2,1,0:T(8,128)S(1)}, f32[4,8,16,256]{3,2,1,0:T(8,128)}, u32[]{:S(2)}) copy-start(f32[4,8,16,256]{3,2,1,0:T(8,128)} %lower.5) | copy-start | bytes 1572868
  0.0 1.2 %copy-start.2 = (f32[5,8,16,256]{3,2,1,0:T(8,128)S(1)}, f32[5,8,16,256]{3,2,1,0:T(8,128)}, u32[]{:S(2)}) copy-start(f32[5,8,16,256]{3,2,1,0:T(8,128)} %adj.3) | copy-start | bytes 1966084
  1.2 0.9 %copy-start.3 = (f32[2,8,16,256]{3,2,1,0:T(8,128)S(1)}, f32[2,8,16,256]{3,2,1,0:T(8,128)}, u32[]{:S(2)}) copy-start(f32[2,8,16,256]{3,2,1,0:T(8,128)} %courant.3) | copy-start | bytes 786436
  2.1 0.9 %copy-start.4 = (f32[2,8,16,256]{3,2,1,0:T(8,128)S(1)}, f32[2,8,16,256]{3,2,1,0:T(8,128)}, u32[]{:S(2)}) copy-start(f32[2,8,16,256]{3,2,1,0:T(8,128)} %metric.3) | copy-start | bytes 786436
  3.2 7.6 %collective-permute-start = (f32[5,2,8,256]{3,2,1,0:T(8,128)S(1)}, f32[5,2,8,256]{3,2,1,0:T(8,128)S(1)}, u32[]{:S(2)}, u32[]{:S(2)}) collective-permute-start(f32[5,2,8,256]{3,2,1,0:T(8,128)S(1)} %get-tuple-element.14), channel_id=1, source_target_pairs={{0,1},{1,0},{2,3},{3,2},{4,5},{5,4},{6,7},{7,6},{8,9},{9,8},{10,11... | collective-permute-start | bytes 245768 | tf_op jit(solution)/shard_map/ppermute | solution.py:236
  3.7 7.8 %copy-start.5 = (f32[4,8,16,256]{3,2,1,0:T(8,128)S(1)}, f32[4,8,16,256]{3,2,1,0:T(8,128)}, u32[]{:S(2)}) copy-start(f32[4,8,16,256]{3,2,1,0:T(8,128)} %pivot.1) | copy-start | bytes 1572868
  3.7 7.8 %collective-permute-start.1 = (f32[5,2,8,256]{3,2,1,0:T(8,128)S(1)}, f32[5,2,8,256]{3,2,1,0:T(8,128)S(1)}, u32[]{:S(2)}, u32[]{:S(2)}) collective-permute-start(f32[5,2,8,256]{3,2,1,0:T(8,128)S(1)} %get-tuple-element.15), channel_id=1, source_target_pairs={{0,15},{1,2},{2,1},{3,4},{4,3},{5,6},{6,5},{7,8},{8,7},{9,10},{10,... | collective-permute-start | bytes 245768 | tf_op jit(solution)/shard_map/ppermute | solution.py:235
  11.6 4.7 %collective-permute-start.2 = (f32[6,16,256]{2,1,0:T(8,128)S(1)}, f32[6,16,256]{2,1,0:T(8,128)S(1)}, u32[]{:S(2)}, u32[]{:S(2)}) collective-permute-start(f32[6,16,256]{2,1,0:T(8,128)S(1)} %get-tuple-element.17.mine), channel_id=1, source_target_pairs={{0,16},{16,0},{1,17},{17,1},{2,18},{18,2},{3,19},{19,3},{4,20},{20... | collective-permute-start | bytes 294920 | tf_op jit(solution)/shard_map/ppermute | solution.py:258
where the time goes:
time: 17.3 us; the launch traced here: 17.1 us
  starting transfers between devices  7.78 us (45%)
  Pallas kernels  3.21 us (19%)
  local copies, waits for them, and re-layouts  3.09 us (18%)
  waiting for transfers between devices  2.97 us (17%)
    ppermute x1, starting transfers between devices, local_pair(): got_far = lax.ppermute(far, 'tile', with_far)  5.67 us
    unnamed x12, local copies, waits for them, and re-layouts  3.09 us
    ppermute x1, waiting for transfers between devices, local_pair(): received = lax.ppermute(summary, 'lev', [(0, 1), (1, 0)])  2.25 us
    ppermute x1, starting transfers between devices, local_pair(): received = lax.ppermute(summary, 'lev', [(0, 1), (1, 0)])  1.6 us
    pallas_call x1, Pallas kernels, local_pair(): pl.pallas_call(inner_body, name='inner', in_specs=[whole()] * 5, out_spec...  1.39 us
    pallas_call x1, Pallas kernels, local_pair(): pl.pallas_call(passive_body, name='passive', in_specs=[whole()] * 3, out_...  0.82 us
    pallas_call x1, Pallas kernels, local_pair(): pl.pallas_call(solve_body, name='solve', in_specs=[whole()] * 5 + [pl.Blo...  0.76 us
    ppermute x1, waiting for transfers between devices, local_pair(): got_far = lax.ppermute(far, 'tile', with_far)  0.71 us
  transfers between devices with their start and end apart: 3, of which 2 were waited for; matrix products, arithmetic and copies ran while one was open for 0% of the time, Pallas kernels for 13%

commit v1 on v0

--- a/solution.py
+++ b/solution.py
@@ -1,3 +1,5 @@
+import functools
+
 import jax
 import jax.numpy as jnp
 from jax import lax
@@ -17,6 +19,14 @@
     return pl.BlockSpec(memory_space=pltpu.VMEM)
 
 
+def in_hbm():
+    return pl.BlockSpec(memory_space=pltpu.HBM)
+
+
+def from_hbm(x):
+    return pltpu.with_memory_space_constraint(x, pltpu.HBM)
+
+
 def params():
     return pltpu.CompilerParams(vmem_limit_bytes=VMEM_LIMIT)
 
@@ -42,32 +52,37 @@
     return tuple(ref[k, level] for k in range(ref.shape[0]))
 
 
-def even_tile():
-    return lax.rem(lax.axis_index("tile"), 2) == 0
-
-
-def edges_body(adj, courant, metric, chip, far):
-    rows = adj.shape[2]
-
-    def emit(out, first):
-        for r in range(2):
-            wind = courant[0, :, first + r, :]
-            for k in range(4):
-                out[k, r] = wind * adj[k, :, first + r, :]
-            out[4, r] = (
-                wind * adj[4, :, first + r, :]
-                + metric[0, :, first + r, :] * adj[0, :, first + r, :]
-            )
-
-    @pl.when(even_tile())
-    def _():
-        emit(chip, rows - 2)
-        emit(far, 0)
-
-    @pl.when(jnp.logical_not(even_tile()))
-    def _():
-        emit(chip, 0)
-        emit(far, rows - 2)
+def edge_rows(rows):
+    return (0, 1, rows - 2, rows - 1)
+
+
+def emit_edges(adj, courant, metric, out, first):
+    for r in range(2):
+        wind = courant[0, :, first + r, :]
+        for k in range(4):
+            out[k, r] = wind * adj[k, :, first + r, :]
+        out[4, r] = wind * adj[4, :, first + r, :]
+        out[5, r] = metric[0, :, first + r, :] * adj[0, :, first + r, :]
+
+
+def fetch_all(sources, targets, sems):
+    copies = [
+        pltpu.make_async_copy(source, target, sems.at[i])
+        for i, (source, target) in enumerate(zip(sources, targets, strict=True))
+    ]
+    for copy in copies:
+        copy.start()
+    return copies
+
+
+def edges_body(
+    adj_in, courant_in, metric_in, ahead, adj, courant, metric, sems
+):
+    for copy in fetch_all(
+        (adj_in, courant_in, metric_in), (adj, courant, metric), sems
+    ):
+        copy.wait()
+    emit_edges(adj, courant, metric, ahead, adj.shape[2] - 2)
 
 
 def across(q):
@@ -89,42 +104,70 @@
     return (8.0 / 12.0) * near - (1.0 / 12.0) * wide
 
 
-def inner_body(adj, courant, metric, lower, upper, passive, active, response):
+def active_body(early, adj, courant, metric, *refs):
+    gains_in = refs[:3]
+    if early:
+        emit_edges(adj, courant, metric, refs[3], 0)
+    summary, active, pivot, lower, upper, sems = refs[-6:]
     levels = adj.shape[1]
-
-    def one(l, _):
-        c0, c1 = courant[0, l], courant[1, l]
-        for k, slot in ((0, 0), (1, 1), (3, 2)):
-            x = adj[k, l]
-            passive[slot, l] = x + across(c0 * x) + along(c1 * x)
-        x = adj[2, l]
-        active[0, l] = x + across(c0 * x) + along(c1 * x)
-        x = adj[4, l]
-        active[1, l] = (
-            x
-            + across(c0 * x + metric[0, l] * adj[0, l])
-            + along(c1 * x + metric[1, l] * adj[1, l])
-        )
-        return 0
-
-    lax.fori_loop(0, levels, one, 0)
-    chain = [at(lower, 0)]
-    for l in range(1, levels):
-        chain.append(matmul(at(lower, l), chain[-1]))
-    total = chain[-1]
-    for l in range(levels - 2, -1, -1):
-        total = add(matmul(at(upper, l), total), chain[l])
-    for k in range(4):
-        response[k] = total[k]
-
-
-def halo_rows(chip, far, field):
-    even = even_tile()
-    got_chip = [chip[field, r] for r in range(2)]
-    got_far = [far[field, r] for r in range(2)]
-    low = [jnp.where(even, b, a) for a, b in zip(got_chip, got_far, strict=True)]
-    high = [jnp.where(even, a, b) for a, b in zip(got_chip, got_far, strict=True)]
-    return low, high
+    here = lax.axis_index("tile") == 0
+
+    @pl.when(here if early else jnp.logical_not(here))
+    def _():
+        copies = fetch_all(gains_in, (lower, upper, pivot), sems)
+
+        def one(l, _):
+            c0, c1 = courant[0, l], courant[1, l]
+            x = adj[2, l]
+            active[0, l] = x + across(c0 * x) + along(c1 * x)
+            x = adj[4, l]
+            active[1, l] = (
+                x
+                + across(c0 * x + metric[0, l] * adj[0, l])
+                + along(c1 * x + metric[1, l] * adj[1, l])
+            )
+            return 0
+
+        lax.fori_loop(0, levels, one, 0)
+        for copy in copies:
+            copy.wait()
+        states = forward(active, pivot, lower)
+
+        @pl.when(lax.axis_index("lev") == 0)
+        def _():
+            for k in range(2):
+                summary[k] = states[-1][k]
+
+        @pl.when(lax.axis_index("lev") == 1)
+        def _():
+            state = backward_first(states, upper)
+            for k in range(2):
+                summary[k] = state[k]
+            chain = [at(lower, 0)]
+            for l in range(1, levels):
+                chain.append(matmul(at(lower, l), chain[-1]))
+            total = chain[-1]
+            for l in range(levels - 2, -1, -1):
+                total = add(matmul(at(upper, l), total), chain[l])
+            for k in range(4):
+                summary[2 + k] = total[k]
+
+
+def forward(active, pivot, lower):
+    states = []
+    for l in range(active.shape[1]):
+        fresh = mul(at(pivot, l), at(active, l))
+        if states:
+            fresh = add(mul(at(lower, l), states[-1]), fresh)
+        states.append(fresh)
+    return states
+
+
+def backward_first(states, upper):
+    state = states[-1]
+    for l in range(len(states) - 2, -1, -1):
+        state = add(mul(at(upper, l), state), states[l])
+    return state
 
 
 def add_halo(ref, slot, low, high):
@@ -138,58 +181,79 @@
     )
 
 
-def sweep_body(active, pivot, lower, upper, response, chip, far, lowered, summary, held_active):
-    levels = active.shape[1]
+def halo_rows(low, high, field):
+    lows = [low[field, r] for r in range(2)]
+    highs = [high[field, r] for r in range(2)]
+    if field == 4:
+        lows = [lows[r] + low[5, r] for r in range(2)]
+        highs = [highs[r] + high[5, r] for r in range(2)]
+    return lows, highs
+
+
+def sweep_body(active, pivot, lower, upper, low, high, lowered, mine, edges, held_active):
+    levels, rows = active.shape[1:3]
     held_active[...] = active[...]
     for slot, field in ((0, 2), (1, 4)):
-        add_halo(held_active, slot, *halo_rows(chip, far, field))
-    states = []
+        add_halo(held_active, slot, *halo_rows(low, high, field))
+    states = forward(held_active, pivot, lower)
     for l in range(levels):
-        fresh = mul(at(pivot, l), at(held_active, l))
-        if states:
-            fresh = add(mul(at(lower, l), states[-1]), fresh)
-        states.append(fresh)
         for k in range(2):
-            lowered[k, l] = fresh[k]
+            lowered[k, l] = states[l][k]
+
+    def emit(state):
+        for k in range(2):
+            mine[k] = state[k]
+            for i, row in enumerate(edge_rows(rows)):
+                edges[pl.ds(4 * k + i, 1)] = state[k][row : row + 1]
 
     @pl.when(lax.axis_index("lev") == 0)
     def _():
-        for k in range(2):
-            summary[k] = states[-1][k]
+        emit(states[-1])
 
     @pl.when(lax.axis_index("lev") == 1)
     def _():
-        state = at(lowered, levels - 1)
-        for l in range(levels - 2, -1, -1):
-            state = add(mul(at(upper, l), state), at(lowered, l))
-        for k in range(2):
-            summary[k] = state[k]
-        for k in range(4):
-            summary[2 + k] = response[k]
-
-
-def passive_body(passive, chip, far, out, held_passive, sems):
-    held_passive[...] = passive[...]
+        emit(backward_first(states, upper))
+
+
+def passive_body(adj, courant, low, high, out, done, sems):
+    levels = adj.shape[1]
     copies = []
+
+    def one(l, _):
+        c0, c1 = courant[0, l], courant[1, l]
+        for slot, field in ((0, 0), (1, 1), (2, 3)):
+            x = adj[field, l]
+            done[slot, l] = x + across(c0 * x) + along(c1 * x)
+        return 0
+
+    lax.fori_loop(0, levels, one, 0)
     for slot, field in ((0, 0), (1, 1), (2, 3)):
-        add_halo(held_passive, slot, *halo_rows(chip, far, field))
+        add_halo(done, slot, *halo_rows(low, high, field))
         copies.append(
-            pltpu.make_async_copy(held_passive.at[slot], out.at[field], sems.at[slot])
+            pltpu.make_async_copy(done.at[slot], out.at[field], sems.at[slot])
         )
         copies[-1].start()
     for copy in copies:
         copy.wait()
 
 
-def solve_body(lowered, lower, upper, mine, summary, partial, out, solved, sems):
+def patched(base, edges, k):
+    rows = base.shape[0]
+    spot = lax.broadcasted_iota(jnp.int32, base.shape, 0)
+    for i, row in enumerate(edge_rows(rows)):
+        base = jnp.where(spot == row, edges[pl.ds(4 * k + i, 1)], base)
+    return base
+
+
+def solve_body(lowered, lower, upper, mine, summary, edges, partial, out, solved, sems):
     del partial
     levels = lowered.shape[1]
+    other = tuple(patched(summary[k], edges, k) for k in range(2))
 
     @pl.when(lax.axis_index("lev") == 0)
     def _():
-        state = (mine[0], mine[1])
         gain = tuple(summary[2 + k] for k in range(4))
-        state = add(mul(gain, state), (summary[0], summary[1]))
+        state = add(mul(gain, (mine[0], mine[1])), other)
         for l in range(levels - 1, -1, -1):
             state = add(mul(at(upper, l), state), at(lowered, l))
             for k in range(2):
@@ -197,7 +261,7 @@
 
     @pl.when(lax.axis_index("lev") == 1)
     def _():
-        entering = (summary[0], summary[1])
+        entering = other
         full = []
         for l in range(levels):
             entering = mul(at(lower, l), entering)
@@ -222,44 +286,72 @@
 def local_pair(adjoint, courant, metric, pivot_inverse, lower_gain, upper_gain):
     fields, levels, rows, cols = adjoint.shape
     tiles = lax.axis_size("tile")
-    chip, far = pl.pallas_call(
+    swap = [(0, 1), (1, 0)]
+    ahead, adj, cour, met = pl.pallas_call(
         edges_body,
         name="edges",
-        in_specs=[whole()] * 3,
-        out_specs=[whole()] * 2,
-        out_shape=[held((fields, 2, levels, cols))] * 2,
-        compiler_params=params(),
-    )(adjoint, courant, metric)
-    with_chip = [(i, i ^ 1) for i in range(tiles)]
-    with_far = [(i, (i - 1 if i % 2 == 0 else i + 1) % tiles) for i in range(tiles)]
-    got_far = lax.ppermute(far, "tile", with_far)
-    got_chip = lax.ppermute(chip, "tile", with_chip)
-    passive, active, response = pl.pallas_call(
-        inner_body,
-        name="inner",
-        in_specs=[whole()] * 5,
+        in_specs=[in_hbm()] * 3,
+        out_specs=[whole()] * 4,
+        out_shape=[
+            held((fields + 1, 2, levels, cols)),
+            held(adjoint.shape),
+            held(courant.shape),
+            held(metric.shape),
+        ],
+        scratch_shapes=[pltpu.SemaphoreType.DMA((3,))],
+        compiler_params=params(),
+    )(from_hbm(adjoint), from_hbm(courant), from_hbm(metric))
+    work = [
+        held((6, rows, cols)),
+        held((2, levels, rows, cols)),
+        held(pivot_inverse.shape),
+        held(lower_gain.shape),
+        held(upper_gain.shape),
+    ]
+    given = (
+        adj, cour, met,
+        from_hbm(lower_gain), from_hbm(upper_gain), from_hbm(pivot_inverse),
+    )
+    low = lax.ppermute(ahead, "tile", [(i, (i + 1) % tiles) for i in range(tiles)])
+    behind, *begun = pl.pallas_call(
+        functools.partial(active_body, True),
+        name="active_first_tile",
+        in_specs=[whole()] * 3 + [in_hbm()] * 3,
+        out_specs=[whole()] * (1 + len(work)),
+        out_shape=[held(ahead.shape)] + work,
+        scratch_shapes=[pltpu.SemaphoreType.DMA((3,))],
+        compiler_params=params(),
+    )(*given)
+    high = lax.ppermute(behind, "tile", [(i, (i - 1) % tiles) for i in range(tiles)])
+    summary, active, pivot, lower, upper = pl.pallas_call(
+        functools.partial(active_body, False),
+        name="active_other_tiles",
+        in_specs=[whole()] * 3 + [in_hbm()] * 3 + [whole()] * len(work),
+        out_specs=[whole()] * len(work),
+        out_shape=work,
+        scratch_shapes=[pltpu.SemaphoreType.DMA((3,))],
+        input_output_aliases={6 + i: i for i in range(len(work))},
+        compiler_params=params(),
+    )(*given, *begun)
+    bulk = lax.ppermute(summary, "lev", swap)
+    lowered, mine, edges = pl.pallas_call(
+        sweep_body,
+        name="sweep",
+        in_specs=[whole()] * 6,
         out_specs=[whole()] * 3,
         out_shape=[
-            held((3, levels, rows, cols)),
             held((2, levels, rows, cols)),
-            held((4, rows, cols)),
+            held((2, rows, cols)),
+            held((8, cols)),
         ],
-        compiler_params=params(),
-    )(adjoint, courant, metric, lower_gain, upper_gain)
-    lowered, summary = pl.pallas_call(
-        sweep_body,
-        name="sweep",
-        in_specs=[whole()] * 7,
-        out_specs=[whole()] * 2,
-        out_shape=[held((2, levels, rows, cols)), held((6, rows, cols))],
         scratch_shapes=[pltpu.VMEM((2, levels, rows, cols), F32)],
         compiler_params=params(),
-    )(active, pivot_inverse, lower_gain, upper_gain, response, got_chip, got_far)
-    received = lax.ppermute(summary, "lev", [(0, 1), (1, 0)])
+    )(active, pivot, lower, upper, low, high)
+    got_edges = lax.ppermute(edges, "lev", swap)
     partial = pl.pallas_call(
         passive_body,
         name="passive",
-        in_specs=[whole()] * 3,
+        in_specs=[whole()] * 4,
         out_specs=pl.BlockSpec(memory_space=pl.ANY),
         out_shape=jax.ShapeDtypeStruct(adjoint.shape, F32),
         scratch_shapes=[
@@ -267,20 +359,20 @@
             pltpu.SemaphoreType.DMA((3,)),
         ],
         compiler_params=params(),
-    )(passive, got_chip, got_far)
+    )(adj, cour, low, high)
     return pl.pallas_call(
         solve_body,
         name="solve",
-        in_specs=[whole()] * 5 + [pl.BlockSpec(memory_space=pl.ANY)],
+        in_specs=[whole()] * 6 + [pl.BlockSpec(memory_space=pl.ANY)],
         out_specs=pl.BlockSpec(memory_space=pl.ANY),
         out_shape=jax.ShapeDtypeStruct(adjoint.shape, F32),
         scratch_shapes=[
             pltpu.VMEM((2, levels, rows, cols), F32),
             pltpu.SemaphoreType.DMA((2,)),
         ],
-        input_output_aliases={5: 0},
-        compiler_params=params(),
-    )(lowered, lower_gain, upper_gain, summary, received, partial)
+        input_output_aliases={6: 0},
+        compiler_params=params(),
+    )(lowered, lower, upper, mine, bulk, got_edges, partial)
 
 
 LEVEL_UNROLL = 16

time: 17.3 us -> 14.2 us (0.82)
  local copies, waits for them, and re-layouts: 3.09 us -> 0 us
  waiting for transfers between devices: 2.97 us -> 0.23 us
  Pallas kernels: 3.21 us -> 5.57 us
  starting transfers between devices: 7.78 us -> 8.17 us
    unnamed x12 -> x0, local copies, waits for them, and re-layouts: 3.09 us -> none
    ppermute x3 -> x4, waiting for transfers between devices: 2.97 us -> 0.23 us  [the longest x1 0.22 us: local_pair(): lax.ppermute(ahead, 'tile', [(i, (i + 1) % tiles) for i in range(tiles)])]
    pallas_call x5 -> x6, Pallas kernels: 3.21 us -> 5.57 us  [the longest x1 1.8 us: local_pair(): pl.pallas_call(passive_body, name='passive', in_specs=[whole()] * 4, out_...]
    ppermute x3 -> x4, starting transfers between devices: 7.78 us -> 8.17 us  [the longest x1 3.64 us: local_pair(): lax.ppermute(behind, 'tile', [(i, (i - 1) % tiles) for i in range(tiles)])]
  transfers between devices with their start and end apart: 3 -> 4, of which waited for: 2 -> 1; matrix products, arithmetic and copies ran while one was open for 0% -> 0% of each run, Pallas kernels for 13% -> 25%
where the time goes in v1:
time: 14.2 us; the launch traced here: 14 us
  starting transfers between devices  8.17 us (58%)
  Pallas kernels  5.57 us (39%)
  waiting for transfers between devices  0.23 us (2%)
    ppermute x1, starting transfers between devices, local_pair(): lax.ppermute(behind, 'tile', [(i, (i - 1) % tiles) for i in range(tiles)])  3.64 us
    ppermute x1, starting transfers between devices, local_pair(): got_edges = lax.ppermute(edges, 'lev', swap)  2.03 us
    ppermute x1, starting transfers between devices, local_pair(): bulk = lax.ppermute(summary, 'lev', swap)  1.98 us
    pallas_call x1, Pallas kernels, local_pair(): pl.pallas_call(passive_body, name='passive', in_specs=[whole()] * 4, out_...  1.8 us
    pallas_call x1, Pallas kernels, local_pair(): pl.pallas_call(functools.partial(active_body, True), name='active_first_t...  1.5 us
    pallas_call x1, Pallas kernels, local_pair(): pl.pallas_call(edges_body, name='edges', in_specs=[in_hbm()] * 3, out_spe...  1.31 us
    pallas_call x1, Pallas kernels, local_pair(): pl.pallas_call(solve_body, name='solve', in_specs=[whole()] * 6 + [pl.Blo...  0.79 us
    ppermute x1, starting transfers between devices, local_pair(): lax.ppermute(ahead, 'tile', [(i, (i + 1) % tiles) for i in range(tiles)])  0.5 us
  transfers between devices with their start and end apart: 4, of which 1 were waited for; matrix products, arithmetic and copies ran while one was open for 0% of the time, Pallas kernels for 25%

profile of v1, /device:TPU:0, one launch (start us, length us, event | category | flops | bytes accessed | tf_op | source)
XLA Modules:
  0.0 14.0 jit_solution(7549063435560725481)
XLA Ops:
  0.0 1.3 %edges.1 = (f32[6,2,8,256]{3,2,1,0:T(8,128)S(1)}, f32[5,8,16,256]{3,2,1,0:T(8,128)S(1)}, f32[2,8,16,256]{3,2,1,0:T(8,128)S(1)}, f32[2,8,16,256]{3,2,1,0:T(8,128)S(1)}) custom-call(f32[5,8,16,256]{3,2,1,0:T(8,128)} %adj_in.1, f32[2,8,16,256]{3,2,1,0:T(8,128)} %courant_in.1, f32[2,8,16,256]{3,2,1,0:T(8,128)} %metric_in.1), custom_call_target="tpu_custom_call" | custom-call | tf_op jit(solution)/shard_map/edges/pallas_call | solution.py:290
  1.3 0.5 %collective-permute-start = (f32[6,2,8,256]{3,2,1,0:T(8,128)S(1)}, f32[6,2,8,256]{3,2,1,0:T(8,128)S(1)}, u32[]{:S(2)}, u32[]{:S(2)}) collective-permute-start(f32[6,2,8,256]{3,2,1,0:T(8,128)S(1)} %get-tuple-element.35), channel_id=1, source_target_pairs={{0,1},{1,2},{2,3},{3,4},{4,5},{5,6},{6,7},{7,8},{8,9},{9,10},{10,1... | collective-permute-start | bytes 294920 | tf_op jit(solution)/shard_map/ppermute | solution.py:315
  1.8 1.5 %active_first_tile.1 = (f32[6,2,8,256]{3,2,1,0:T(8,128)S(1)}, f32[6,16,256]{2,1,0:T(8,128)S(1)}, f32[2,8,16,256]{3,2,1,0:T(8,128)S(1)}, f32[4,8,16,256]{3,2,1,0:...) custom-call(f32[5,8,16,256]{3,2,1,0:T(8,128)S(1)} %get-tuple-element.23.adj, ...), custom_call_target="tpu_custom_call" | custom-call | tf_op jit(solution)/shard_map/active_first_tile/pallas_call | solution.py:316
  3.3 3.6 %collective-permute-start.1 = (f32[6,2,8,256]{3,2,1,0:T(8,128)S(1)}, f32[6,2,8,256]{3,2,1,0:T(8,128)S(1)}, u32[]{:S(2)}, u32[]{:S(2)}) collective-permute-start(f32[6,2,8,256]{3,2,1,0:T(8,128)S(1)} %get-tuple-element.36), channel_id=1, source_target_pairs={{0,15},{1,0},{2,1},{3,2},{4,3},{5,4},{6,5},{7,6},{8,7},{9,8},{10,9... | collective-permute-start | bytes 294920 | tf_op jit(solution)/shard_map/ppermute | solution.py:325
  7.0 2.0 %collective-permute-start.2 = (f32[6,16,256]{2,1,0:T(8,128)S(1)}, f32[6,16,256]{2,1,0:T(8,128)S(1)}, u32[]{:S(2)}, u32[]{:S(2)}) collective-permute-start(f32[6,16,256]{2,1,0:T(8,128)S(1)} %get-tuple-element.39), channel_id=1, source_target_pairs={{0,16},{16,0},{1,17},{17,1},{2,18},{18,2},{3,19},{19,3},{4,20},{20... | collective-permute-start | bytes 294920 | tf_op jit(solution)/shard_map/ppermute | solution.py:336
  9.0 0.2 %collective-permute-done.low = f32[6,2,8,256]{3,2,1,0:T(8,128)S(1)} collective-permute-done((f32[6,2,8,256]{3,2,1,0:T(8,128)S(1)}, f32[6,2,8,256]{3,2,1,0:T(8,128)S(1)}, u32[]{:S(2)}, u32[]{:S(2)}) %collective-permute-start) | collective-permute-done | bytes 98336 | tf_op jit(solution)/shard_map/ppermute | solution.py:315
  9.2 0.0 collective-permute-done.1.high
  9.2 0.1 sweep.1
  9.4 2.0 %collective-permute-start.3 = (f32[8,256]{1,0:T(8,128)S(1)}, f32[8,256]{1,0:T(8,128)S(1)}, u32[]{:S(2)}, u32[]{:S(2)}) collective-permute-start(f32[8,256]{1,0:T(8,128)S(1)} %get-tuple-element.40), channel_id=1, source_target_pairs={{0,16},{16,0},{1,17},{17,1},{2,18},{18,2},{3,19},{19,3},{4,20},{20... | collective-permute-start | bytes 24584 | tf_op jit(solution)/shard_map/ppermute | solution.py:350
  11.4 1.8 %passive.1.partial = f32[5,8,16,256]{3,2,1,0:T(8,128)} custom-call(f32[5,8,16,256]{3,2,1,0:T(8,128)S(1)} %get-tuple-element.23.adj, f32[2,8,16,256]{3,2,1,0:T(8,128)S(1)} %get-tuple-element.24.courant, f32[6,2,8,256]{3,2,1,0:T(8,128)S(1)} %collective-permute-done.low, f32[6,2,8,256]{3,2,1,0:T(8,128)S(1)} %collective-permute-done.1.high), custom_call_target="tpu_custom_call" | custom-call | tf_op jit(solution)/shard_map/passive/pallas_call | solution.py:351
  13.2 0.0 collective-permute-done.2.summary
  13.2 0.0 collective-permute-done.3.edges
  13.2 0.8 %solve.1 = f32[5,8,16,256]{3,2,1,0:T(8,128)} custom-call(f32[2,8,16,256]{3,2,1,0:T(8,128)S(1)} %get-tuple-element.37.lowered, f32[4,8,16,256]{3,2,1,0:T(8,128)S(1)} %get-tuple-element.33.lower, f32[4,8,16,256]{3,2,1,0:T(8,128)S(1)} %get-tuple-element.34.upper, f32[2,16,256]{2,1,0:T(8,128)S(1)} %get-tuple-element.38.mine, ...), custom_call_target="tpu_custom_call", output_to_operand_aliasing={{}: (6, {})} | custom-call | tf_op jit(solution)/shard_map/solve/pallas_call | solution.py:363
  (1 shorter events, 0.0 us)
Async XLA Ops:
  1.3 7.9 %collective-permute-start = (f32[6,2,8,256]{3,2,1,0:T(8,128)S(1)}, f32[6,2,8,256]{3,2,1,0:T(8,128)S(1)}, u32[]{:S(2)}, u32[]{:S(2)}) collective-permute-start(f32[6,2,8,256]{3,2,1,0:T(8,128)S(1)} %get-tuple-element.35), channel_id=1, source_target_pairs={{0,1},{1,2},{2,3},{3,4},{4,5},{5,6},{6,7},{7,8},{8,9},{9,10},{10,1... | collective-permute-start | bytes 294920 | tf_op jit(solution)/shard_map/ppermute | solution.py:315
  3.3 5.9 %collective-permute-start.1 = (f32[6,2,8,256]{3,2,1,0:T(8,128)S(1)}, f32[6,2,8,256]{3,2,1,0:T(8,128)S(1)}, u32[]{:S(2)}, u32[]{:S(2)}) collective-permute-start(f32[6,2,8,256]{3,2,1,0:T(8,128)S(1)} %get-tuple-element.36), channel_id=1, source_target_pairs={{0,15},{1,0},{2,1},{3,2},{4,3},{5,4},{6,5},{7,6},{8,7},{9,8},{10,9... | collective-permute-start | bytes 294920 | tf_op jit(solution)/shard_map/ppermute | solution.py:325
  7.0 6.2 %collective-permute-start.2 = (f32[6,16,256]{2,1,0:T(8,128)S(1)}, f32[6,16,256]{2,1,0:T(8,128)S(1)}, u32[]{:S(2)}, u32[]{:S(2)}) collective-permute-start(f32[6,16,256]{2,1,0:T(8,128)S(1)} %get-tuple-element.39), channel_id=1, source_target_pairs={{0,16},{16,0},{1,17},{17,1},{2,18},{18,2},{3,19},{19,3},{4,20},{20... | collective-permute-start | bytes 294920 | tf_op jit(solution)/shard_map/ppermute | solution.py:336
  9.4 3.9 %collective-permute-start.3 = (f32[8,256]{1,0:T(8,128)S(1)}, f32[8,256]{1,0:T(8,128)S(1)}, u32[]{:S(2)}, u32[]{:S(2)}) collective-permute-start(f32[8,256]{1,0:T(8,128)S(1)} %get-tuple-element.40), channel_id=1, source_target_pairs={{0,16},{16,0},{1,17},{17,1},{2,18},{18,2},{3,19},{19,3},{4,20},{20... | collective-permute-start | bytes 24584 | tf_op jit(solution)/shard_map/ppermute | solution.py:350

commit v2 on v1

v2 whole, which is shorter than its diff:
```python
import jax
import jax.numpy as jnp
from jax import lax
from jax.experimental import pallas as pl
from jax.experimental.pallas import tpu as pltpu
from jax.sharding import PartitionSpec as P

F32 = jnp.float32
VMEM_LIMIT = 24 * 1024 * 1024


def held(shape):
    return pltpu.VMEM(shape, F32)


def whole():
    return pl.BlockSpec(memory_space=pltpu.VMEM)


def in_hbm():
    return pl.BlockSpec(memory_space=pltpu.HBM)


def from_hbm(x):
    return pltpu.with_memory_space_constraint(x, pltpu.HBM)


def params():
    return pltpu.CompilerParams(vmem_limit_bytes=VMEM_LIMIT)


def mul(m, v):
    return (m[0] * v[0] + m[1] * v[1], m[2] * v[0] + m[3] * v[1])


def matmul(m, n):
    return (
        m[0] * n[0] + m[1] * n[2],
        m[0] * n[1] + m[1] * n[3],
        m[2] * n[0] + m[3] * n[2],
        m[2] * n[1] + m[3] * n[3],
    )


def add(a, b):
    return tuple(x + y for x, y in zip(a, b, strict=True))


def at(ref, level):
    return tuple(ref[k, level] for k in range(ref.shape[0]))


def emit_edges(adj, courant, metric, out, first):
    for r in range(2):
        row = first + r
        wind = courant[0, :, row, :]
        for k in range(4):
            out[k, r] = wind * adj[k, :, row, :]
        out[4, r] = wind * adj[4, :, row, :] + metric[0, :, row, :] * adj[0, :, row, :]


def fetch_all(sources, targets, sems):
    copies = [
        pltpu.make_async_copy(source, target, sems.at[i])
        for i, (source, target) in enumerate(zip(sources, targets, strict=True))
    ]
    for copy in copies:
        copy.start()
    return copies


def tail_rows(ref):
    return ref.at[:, :, pl.ds(ref.shape[2] - 8, 8)]


def head_rows(ref):
    return ref.at[:, :, pl.ds(0, ref.shape[2] - 8)]


def edges_body(
    adj_in, courant_in, metric_in, ahead, adj, courant, metric, sems
):
    first = lax.axis_index("tile") == 0
    given, targets = (adj_in, courant_in, metric_in), (adj, courant, metric)

    @pl.when(first)
    def _():
        for copy in fetch_all(map(tail_rows, given), map(tail_rows, targets), sems):
            copy.wait()

    @pl.when(jnp.logical_not(first))
    def _():
        for copy in fetch_all(given, targets, sems):
            copy.wait()

    emit_edges(adj, courant, metric, ahead, adj.shape[2] - 2)


def across(q):
    rows = q.shape[0]
    spot = lax.broadcasted_iota(jnp.int32, q.shape, 0)
    out = None
    for step, weight in ((1, 8.0 / 12.0), (2, -1.0 / 12.0)):
        ahead = jnp.where(spot < rows - step, pltpu.roll(q, rows - step, 0), 0.0)
        behind = jnp.where(spot >= step, pltpu.roll(q, step, 0), 0.0)
        term = weight * (ahead - behind)
        out = term if out is None else out + term
    return out


def along(q):
    cols = q.shape[1]
    near = pltpu.roll(q, cols - 1, 1) - pltpu.roll(q, 1, 1)
    wide = pltpu.roll(q, cols - 2, 1) - pltpu.roll(q, 2, 1)
    return (8.0 / 12.0) * near - (1.0 / 12.0) * wide


def passive_base(adj, courant, passive):
    def one(l, _):
        c0, c1 = courant[0, l], courant[1, l]
        for slot, field in ((0, 0), (1, 1), (2, 3)):
            x = adj[field, l]
            passive[slot, l] = x + across(c0 * x) + along(c1 * x)
        return 0

    lax.fori_loop(0, adj.shape[1], one, 0)


def first_tile_body(adj_in, courant_in, metric_in, lower_in, upper_in, pivot_in, *refs):
    behind, adj, courant, metric, *work = refs[3:-2]
    sems, head_sems = refs[-2:]
    first = lax.axis_index("tile") == 0

    @pl.when(first)
    def _():
        heads = fetch_all(
            map(head_rows, (adj_in, courant_in, metric_in)),
            map(head_rows, (adj, courant, metric)),
            head_sems,
        )
        gains = fetch_all((lower_in, upper_in, pivot_in), work[-2:] + work[-3:-2], sems)
        for copy in heads:
            copy.wait()
        active_base(adj, courant, metric, work[1])
        summarise(work, gains)

    emit_edges(adj, courant, metric, behind, 0)


def other_tiles_body(adj, courant, metric, lower_in, upper_in, pivot_in, *refs):
    *work, sems = refs[-6:]

    @pl.when(lax.axis_index("tile") > 0)
    def _():
        gains = fetch_all((lower_in, upper_in, pivot_in), work[-2:] + work[-3:-2], sems)
        active_base(adj, courant, metric, work[1])
        summarise(work, gains)


def active_base(adj, courant, metric, active):
    def one(l, _):
        c0, c1 = courant[0, l], courant[1, l]
        x = adj[2, l]
        active[0, l] = x + across(c0 * x) + along(c1 * x)
        x = adj[4, l]
        active[1, l] = (
            x
            + across(c0 * x + metric[0, l] * adj[0, l])
            + along(c1 * x + metric[1, l] * adj[1, l])
        )
        return 0

    lax.fori_loop(0, adj.shape[1], one, 0)


def summarise(work, gains):
    bulk, active, pivot, lower, upper = work
    levels = active.shape[1]
    for copy in gains:
        copy.wait()
    states = forward(active, pivot, lower)

    rows = active.shape[2]

    def emit(state):
        for k in range(2):
            start = 4 * rows + k * (rows - 8)
            bulk[pl.ds(start, rows - 8)] = state[k][4 : rows - 4]

    @pl.when(lax.axis_index("lev") == 0)
    def _():
        emit(states[-1])

    @pl.when(lax.axis_index("lev") == 1)
    def _():
        emit(backward_first(states, upper))
        chain = [at(lower, 0)]
        for l in range(1, levels):
            chain.append(matmul(at(lower, l), chain[-1]))
        total = chain[-1]
        for l in range(levels - 2, -1, -1):
            total = add(matmul(at(upper, l), total), chain[l])
        for k in range(4):
            bulk[pl.ds(k * rows, rows)] = total[k]


def forward(active, pivot, lower):
    states = []
    for l in range(active.shape[1]):
        fresh = mul(at(pivot, l), at(active, l))
        if states:
            fresh = add(mul(at(lower, l), states[-1]), fresh)
        states.append(fresh)
    return states


def backward_first(states, upper):
    state = states[-1]
    for l in range(len(states) - 2, -1, -1):
        state = add(mul(at(upper, l), state), states[l])
    return state


def add_halo(ref, slot, low, high):
    rows = ref.shape[2]
    near, wide = 8.0 / 12.0, 1.0 / 12.0
    ref[slot, :, 0, :] = ref[slot, :, 0, :] + (wide * low[0] - near * low[1])
    ref[slot, :, 1, :] = ref[slot, :, 1, :] + wide * low[1]
    ref[slot, :, rows - 2, :] = ref[slot, :, rows - 2, :] - wide * high[0]
    ref[slot, :, rows - 1, :] = ref[slot, :, rows - 1, :] + (
        near * high[0] - wide * high[1]
    )


def halo_rows(low, high, field):
    return [[ref[field, r] for r in range(2)] for ref in (low, high)]


def sweep_body(given, pivot, lower, upper, low, high, base, lowered, mine, edges, active, kept):
    del given, base, kept
    levels, rows = active.shape[1:3]
    for slot, field in ((0, 2), (1, 4)):
        add_halo(active, slot, *halo_rows(low, high, field))
    states = forward(active, pivot, lower)
    for l in range(levels):
        for k in range(2):
            lowered[k, l] = states[l][k]

    def emit(state):
        for k in range(2):
            mine[k] = state[k]
            edges[pl.ds(8 * k, 4)] = state[k][:4]
            edges[pl.ds(8 * k + 4, 4)] = state[k][rows - 4 :]

    @pl.when(lax.axis_index("lev") == 0)
    def _():
        emit(states[-1])

    @pl.when(lax.axis_index("lev") == 1)
    def _():
        emit(backward_first(states, upper))


def odd_tiles_body(adj, courant, passive):
    @pl.when(lax.rem(lax.axis_index("tile"), 2) == 1)
    def _():
        passive_base(adj, courant, passive)


def passive_body(adj, courant, base, low, high, out, passive, sems):
    del base

    @pl.when(lax.rem(lax.axis_index("tile"), 2) == 0)
    def _():
        passive_base(adj, courant, passive)

    copies = []
    for slot, field in enumerate((0, 1, 3)):
        add_halo(passive, slot, *halo_rows(low, high, field))
        copies.append(
            pltpu.make_async_copy(passive.at[slot], out.at[field], sems.at[slot])
        )
        copies[-1].start()
    for copy in copies:
        copy.wait()


def solve_body(
    lowered, lower, upper, mine, bulk, edges, partial, out, solved, other, sems
):
    del partial
    levels, rows = lowered.shape[1:3]
    half = levels // 2
    for k in range(2):
        other[k, pl.ds(0, 4)] = edges[pl.ds(8 * k, 4)]
        other[k, pl.ds(4, rows - 8)] = bulk[pl.ds(4 * rows + k * (rows - 8), rows - 8)]
        other[k, pl.ds(rows - 4, 4)] = edges[pl.ds(8 * k + 4, 4)]

    def copies(part):
        span = pl.ds(part * half, half)
        return [
            pltpu.make_async_copy(
                solved.at[k, span], out.at[field, span], sems.at[part, k]
            )
            for k, field in ((0, 2), (1, 4))
        ]

    def descend(state, full):
        for l in range(levels - 1, -1, -1):
            if state is None:
                state = full(l)
            else:
                state = add(mul(at(upper, l), state), full(l))
            for k in range(2):
                solved[k, l] = state[k]
            if l == half or l == 0:
                for copy in copies(l // half):
                    copy.start()

    @pl.when(lax.axis_index("lev") == 0)
    def _():
        gain = tuple(bulk[pl.ds(k * rows, rows)] for k in range(4))
        descend(
            add(mul(gain, (mine[0], mine[1])), (other[0], other[1])),
            lambda l: at(lowered, l),
        )

    @pl.when(lax.axis_index("lev") == 1)
    def _():
        entering = (other[0], other[1])
        full = []
        for l in range(levels):
            entering = mul(at(lower, l), entering)
            full.append(add(entering, at(lowered, l)))
        descend(None, lambda l: full[l])

    for part in range(2):
        for copy in copies(part):
            copy.wait()


def local_pair(adjoint, courant, metric, pivot_inverse, lower_gain, upper_gain):
    fields, levels, rows, cols = adjoint.shape
    tiles = lax.axis_size("tile")
    swap = [(0, 1), (1, 0)]
    forth = [(i, (i + 1) % tiles) for i in range(tiles)]
    back = [(i, (i - 1) % tiles) for i in range(tiles)]
    halo = held((fields, 2, levels, cols))
    inputs = [held(adjoint.shape), held(courant.shape), held(metric.shape)]
    sems = pltpu.SemaphoreType.DMA((3,))
    sources = (from_hbm(adjoint), from_hbm(courant), from_hbm(metric))
    gains = (from_hbm(lower_gain), from_hbm(upper_gain), from_hbm(pivot_inverse))
    ahead, *fetched = pl.pallas_call(
        edges_body,
        name="edges",
        in_specs=[in_hbm()] * 3,
        out_specs=[whole()] * 4,
        out_shape=[halo] + inputs,
        scratch_shapes=[sems],
        compiler_params=params(),
    )(*sources)
    work = [
        held((6 * rows - 16, cols)),
        held((2, levels, rows, cols)),
        held(pivot_inverse.shape),
        held(lower_gain.shape),
        held(upper_gain.shape),
    ]
    low = lax.ppermute(ahead, "tile", forth)
    behind, adj, cour, met, *begun = pl.pallas_call(
        first_tile_body,
        name="first_tile",
        in_specs=[in_hbm()] * 6 + [whole()] * 3,
        out_specs=[whole()] * (4 + len(work)),
        out_shape=[halo] + inputs + work,
        scratch_shapes=[sems, sems],
        input_output_aliases={6 + i: 1 + i for i in range(3)},
        compiler_params=params(),
    )(*sources, *gains, *fetched)
    high = lax.ppermute(behind, "tile", back)
    summary, active, pivot, lower, upper = pl.pallas_call(
        other_tiles_body,
        name="other_tiles",
        in_specs=[whole()] * 3 + [in_hbm()] * 3 + [whole()] * len(work),
        out_specs=[whole()] * len(work),
        out_shape=work,
        scratch_shapes=[sems],
        input_output_aliases={6 + i: i for i in range(len(work))},
        compiler_params=params(),
    )(adj, cour, met, *gains, *begun)
    bulk = lax.ppermute(summary, "lev", swap)
    base = pl.pallas_call(
        odd_tiles_body,
        name="odd_tiles",
        in_specs=[whole()] * 2,
        out_specs=whole(),
        out_shape=held((3, levels, rows, cols)),
        compiler_params=params(),
    )(adj, cour)
    lowered, mine, edges, _, base = pl.pallas_call(
        sweep_body,
        name="sweep",
        in_specs=[whole()] * 7,
        out_specs=[whole()] * 5,
        out_shape=[
            held((2, levels, rows, cols)),
            held((2, rows, cols)),
            held((16, cols)),
            work[1],
            held((3, levels, rows, cols)),
        ],
        input_output_aliases={0: 3, 6: 4},
        compiler_params=params(),
    )(active, pivot, lower, upper, low, high, base)
    got_edges = lax.ppermute(edges, "lev", swap)
    partial, _ = pl.pallas_call(
        passive_body,
        name="passive",
        in_specs=[whole()] * 5,
        out_specs=[pl.BlockSpec(memory_space=pl.ANY), whole()],
        out_shape=[
            jax.ShapeDtypeStruct(adjoint.shape, F32),
            held((3, levels, rows, cols)),
        ],
        scratch_shapes=[sems],
        input_output_aliases={2: 1},
        compiler_params=params(),
    )(adj, cour, base, low, high)
    return pl.pallas_call(
        solve_body,
        name="solve",
        in_specs=[whole()] * 6 + [pl.BlockSpec(memory_space=pl.ANY)],
        out_specs=pl.BlockSpec(memory_space=pl.ANY),
        out_shape=jax.ShapeDtypeStruct(adjoint.shape, F32),
        scratch_shapes=[
            pltpu.VMEM((2, levels, rows, cols), F32),
            pltpu.VMEM((2, rows, cols), F32),
            pltpu.SemaphoreType.DMA((2, 2)),
        ],
        input_output_aliases={6: 0},
        compiler_params=params(),
    )(lowered, lower, upper, mine, bulk, got_edges, partial)


LEVEL_UNROLL = 16


def with_halo(block, sides, width):
    for axis, dim in sides:
        count = lax.axis_size(axis)
        forward = [(i, i + 1) for i in range(count - 1)]
        forward.append((count - 1, 0))
        backward = [(target, source) for source, target in forward]
        low = lax.ppermute(
            lax.slice_in_dim(block, block.shape[dim] - width, None, axis=dim), axis, forward
        )
        high = lax.ppermute(lax.slice_in_dim(block, 0, width, axis=dim), axis, backward)
        block = jnp.concatenate([low, block, high], axis=dim)
    return block


def centered_roll(values, axis_id):
    ahead_one = jnp.roll(values, -1, axis_id)
    behind_one = jnp.roll(values, 1, axis_id)
    ahead_two = jnp.roll(values, -2, axis_id)
    behind_two = jnp.roll(values, 2, axis_id)
    return (8.0 * (ahead_one - behind_one) - (ahead_two - behind_two)) / 12.0


def centered_padded(padded):
    ahead_one = padded[:, :, 3:-1, :]
    behind_one = padded[:, :, 1:-3, :]
    ahead_two = padded[:, :, 4:, :]
    behind_two = padded[:, :, :-4, :]
    return (8.0 * (ahead_one - behind_one) - (ahead_two - behind_two)) / 12.0


def mat_vec(system_matrix, vector):
    return jnp.stack(
        [
            system_matrix[0] * vector[0] + system_matrix[1] * vector[1],
            system_matrix[2] * vector[0] + system_matrix[3] * vector[1],
        ]
    )


def chain_run(coupling, forcing, initial, backward):

    def advance(state, inputs):
        fresh = mat_vec(inputs[0], state) + inputs[1]
        return (fresh, fresh)

    final_state, states = lax.scan(
        advance,
        initial,
        (jnp.moveaxis(coupling, 1, 0), jnp.moveaxis(forcing, 1, 0)),
        reverse=backward,
        unroll=min(LEVEL_UNROLL, coupling.shape[1]),
    )
    return jnp.moveaxis(states, 0, 1)


def column_solve(pieces):
    forcing, lower_part, upper_part = pieces
    initial = jnp.zeros((2,) + forcing.shape[2:], jnp.float32)
    lowered = chain_run(lower_part, forcing, initial, False)
    solved = chain_run(upper_part, lowered, initial, True)
    return lax.all_to_all(solved, "lev", split_axis=1, concat_axis=2, tiled=True)


def local_any(adjoint, courant, metric, pivot_inverse, lower_gain, upper_gain):
    weighted = jnp.concatenate([courant[0] * adjoint, (metric[0] * adjoint[0])[None]], 0)
    padded = with_halo(weighted, (("tile", 2),), 2)
    across = centered_padded(padded)
    advected = adjoint + across[:5] + centered_roll(courant[1] * adjoint, 3)
    pressure_field = advected[4] + across[5] + centered_roll(metric[1] * adjoint[1], 2)
    forcing = mat_vec(pivot_inverse, jnp.stack([advected[2], pressure_field]))
    solved = column_solve(
        (
            lax.all_to_all(forcing, "lev", split_axis=2, concat_axis=1, tiled=True),
            lax.all_to_all(lower_gain, "lev", split_axis=2, concat_axis=1, tiled=True),
            lax.all_to_all(upper_gain, "lev", split_axis=2, concat_axis=1, tiled=True),
        )
    )
    return jnp.stack([advected[0], advected[1], solved[0], advected[3], solved[1]])


def solution(mesh):
    placed = (P(None, "lev", "tile", None),) * 6
    pair = mesh.shape["lev"] == 2 and mesh.shape["tile"] % 2 == 0
    return jax.shard_map(
        local_pair if pair else local_any,
        mesh=mesh,
        in_specs=placed,
        out_specs=P(None, "lev", "tile", None),
        check_vma=False,
    )
```

time: 14.2 us -> 13.9 us (0.979)
  starting transfers between devices: 8.17 us -> 7.11 us
  Pallas kernels: 5.57 us -> 6.26 us
    pallas_call x4 -> x5, Pallas kernels: 3.47 us -> 4.34 us  [the longest x1 2.4 us: local_pair(): pl.pallas_call(first_tile_body, name='first_tile', in_specs=[in_hbm()] *...]
    ppermute x2, starting transfers between devices: 4.15 us -> 3.46 us  [the longest x1 2.79 us: local_pair(): high = lax.ppermute(behind, 'tile', back)]
    ppermute x1, starting transfers between devices: 2.03 us -> 1.84 us  [local_pair(): got_edges = lax.ppermute(edges, 'lev', swap)]
    ppermute x1, starting transfers between devices: 1.98 us -> 1.81 us  [local_pair(): bulk = lax.ppermute(summary, 'lev', swap)]
    pallas_call x1, Pallas kernels: 1.31 us -> 1.15 us  [local_pair(): pl.pallas_call(edges_body, name='edges', in_specs=[in_hbm()] * 3, out_spe...]
  transfers between devices with their start and end apart: 4 -> 4, of which waited for: 1 -> 2; matrix products, arithmetic and copies ran while one was open for 0% -> 0% of each run, Pallas kernels for 25% -> 31%
where the time goes in v2:
time: 13.9 us; the launch traced here: 13.8 us
  starting transfers between devices  7.11 us (51%)
  Pallas kernels  6.26 us (45%)
  waiting for transfers between devices  0.36 us (3%)
    ppermute x1, starting transfers between devices, local_pair(): high = lax.ppermute(behind, 'tile', back)  2.79 us
    pallas_call x1, Pallas kernels, local_pair(): pl.pallas_call(first_tile_body, name='first_tile', in_specs=[in_hbm()] *...  2.4 us
    ppermute x1, starting transfers between devices, local_pair(): got_edges = lax.ppermute(edges, 'lev', swap)  1.84 us
    ppermute x1, starting transfers between devices, local_pair(): bulk = lax.ppermute(summary, 'lev', swap)  1.81 us
    pallas_call x1, Pallas kernels, local_pair(): pl.pallas_call(passive_body, name='passive', in_specs=[whole()] * 5, out_...  1.8 us
    pallas_call x1, Pallas kernels, local_pair(): pl.pallas_call(edges_body, name='edges', in_specs=[in_hbm()] * 3, out_spe...  1.15 us
    pallas_call x1, Pallas kernels, local_pair(): pl.pallas_call(solve_body, name='solve', in_specs=[whole()] * 6 + [pl.Blo...  0.76 us
    ppermute x1, starting transfers between devices, local_pair(): low = lax.ppermute(ahead, 'tile', forth)  0.66 us
  transfers between devices with their start and end apart: 4, of which 2 were waited for; matrix products, arithmetic and copies ran while one was open for 0% of the time, Pallas kernels for 31%

profile of v2, /device:TPU:0, one launch (start us, length us, event | category | flops | bytes accessed | tf_op | source)
XLA Modules:
  0.0 13.8 jit_solution(63741802957063356)
XLA Ops:
  0.0 1.2 %edges.1 = (f32[5,2,8,256]{3,2,1,0:T(8,128)S(1)}, f32[5,8,16,256]{3,2,1,0:T(8,128)S(1)}, f32[2,8,16,256]{3,2,1,0:T(8,128)S(1)}, f32[2,8,16,256]{3,2,1,0:T(8,128)S(1)}) custom-call(f32[5,8,16,256]{3,2,1,0:T(8,128)} %adj_in.3, f32[2,8,16,256]{3,2,1,0:T(8,128)} %courant_in.3, f32[2,8,16,256]{3,2,1,0:T(8,128)} %metric_in.3), custom_call_target="tpu_custom_call" | custom-call | tf_op jit(solution)/shard_map/edges/pallas_call | solution.py:353
  1.2 0.7 %collective-permute-start = (f32[5,2,8,256]{3,2,1,0:T(8,128)S(1)}, f32[5,2,8,256]{3,2,1,0:T(8,128)S(1)}, u32[]{:S(2)}, u32[]{:S(2)}) collective-permute-start(f32[5,2,8,256]{3,2,1,0:T(8,128)S(1)} %get-tuple-element.43), channel_id=1, source_target_pairs={{0,1},{1,2},{2,3},{3,4},{4,5},{5,6},{6,7},{7,8},{8,9},{9,10},{10,1... | collective-permute-start | bytes 245768 | tf_op jit(solution)/shard_map/ppermute | solution.py:369
  1.8 2.4 %first_tile.1 = (f32[5,2,8,256]{3,2,1,0:T(8,128)S(1)}, f32[5,8,16,256]{3,2,1,0:T(8,128)S(1)}, f32[2,8,16,256]{3,2,1,0:T(8,128)S(1)}, f32[2,8,16,256]{3,2,1,0:T(8...) custom-call(f32[5,8,16,256]{3,2,1,0:T(8,128)} %adj_in.3, ...), custom_call_target="tpu_custom_call", output_to_operand_aliasing={{1}: (6, {}), {2}: (7, {}), {3}: (8, {})} | custom-call | tf_op jit(solution)/shard_map/first_tile/pallas_call | solution.py:370
  4.2 2.8 %collective-permute-start.1 = (f32[5,2,8,256]{3,2,1,0:T(8,128)S(1)}, f32[5,2,8,256]{3,2,1,0:T(8,128)S(1)}, u32[]{:S(2)}, u32[]{:S(2)}) collective-permute-start(f32[5,2,8,256]{3,2,1,0:T(8,128)S(1)} %get-tuple-element.44), channel_id=1, source_target_pairs={{0,15},{1,0},{2,1},{3,2},{4,3},{5,4},{6,5},{7,6},{8,7},{9,8},{10,9... | collective-permute-start | bytes 245768 | tf_op jit(solution)/shard_map/ppermute | solution.py:380
  7.1 1.8 %collective-permute-start.2 = (f32[80,256]{1,0:T(8,128)S(1)}, f32[80,256]{1,0:T(8,128)S(1)}, u32[]{:S(2)}, u32[]{:S(2)}) collective-permute-start(f32[80,256]{1,0:T(8,128)S(1)} %get-tuple-element.47), channel_id=1, source_target_pairs={{0,16},{16,0},{1,17},{17,1},{2,18},{18,2},{3,19},{19,3},{4,20},{20... | collective-permute-start | bytes 245768 | tf_op jit(solution)/shard_map/ppermute | solution.py:391
  8.9 0.2 %collective-permute-done.low = f32[5,2,8,256]{3,2,1,0:T(8,128)S(1)} collective-permute-done((f32[5,2,8,256]{3,2,1,0:T(8,128)S(1)}, f32[5,2,8,256]{3,2,1,0:T(8,128)S(1)}, u32[]{:S(2)}, u32[]{:S(2)}) %collective-permute-start) | collective-permute-done | bytes 81952 | tf_op jit(solution)/shard_map/ppermute | solution.py:369
  9.0 0.0 collective-permute-done.1.high
  9.1 0.1 sweep.1
  9.2 1.8 %collective-permute-start.3 = (f32[16,256]{1,0:T(8,128)S(1)}, f32[16,256]{1,0:T(8,128)S(1)}, u32[]{:S(2)}, u32[]{:S(2)}) collective-permute-start(f32[16,256]{1,0:T(8,128)S(1)} %get-tuple-element.48), channel_id=1, source_target_pairs={{0,16},{16,0},{1,17},{17,1},{2,18},{18,2},{3,19},{19,3},{4,20},{20... | collective-permute-start | bytes 49160 | tf_op jit(solution)/shard_map/ppermute | solution.py:415
  11.1 1.8 %passive.1 = (f32[5,8,16,256]{3,2,1,0:T(8,128)}, f32[3,8,16,256]{3,2,1,0:T(8,128)S(1)}) custom-call(f32[5,8,16,256]{3,2,1,0:T(8,128)S(1)} %get-tuple-element.31.adj, f32[2,8,16,256]{3,2,1,0:T(8,128)S(1)} %get-tuple-element.32.courant, f32[3,8,16,256]{3,2,1,0:T(8,128)S(1)} %get-tuple-element.49.base, ...), custom_call_target="tpu_custom_call", output_to_operand_aliasing={{1}: (2, {})} | custom-call | tf_op jit(solution)/shard_map/passive/pallas_call | solution.py:416
  12.9 0.0 collective-permute-done.2.bulk
  12.9 0.1 %collective-permute-done.3.edges = f32[16,256]{1,0:T(8,128)S(1)} collective-permute-done((f32[16,256]{1,0:T(8,128)S(1)}, f32[16,256]{1,0:T(8,128)S(1)}, u32[]{:S(2)}, u32[]{:S(2)}) %collective-permute-start.3) | collective-permute-done | bytes 16416 | tf_op jit(solution)/shard_map/ppermute | solution.py:415
  13.0 0.8 %solve.1 = f32[5,8,16,256]{3,2,1,0:T(8,128)} custom-call(f32[2,8,16,256]{3,2,1,0:T(8,128)S(1)} %get-tuple-element.45.lowered, f32[4,8,16,256]{3,2,1,0:T(8,128)S(1)} %get-tuple-element.41.lower, f32[4,8,16,256]{3,2,1,0:T(8,128)S(1)} %get-tuple-element.42.upper, f32[2,16,256]{2,1,0:T(8,128)S(1)} %get-tuple-element.46.mine, ...), custom_call_target="tpu_custom_call", output_to_operand_aliasing={{}: (6, {})} | custom-call | tf_op jit(solution)/shard_map/solve/pallas_call | solution.py:429
  (2 shorter events, 0.0 us)
Async XLA Ops:
  1.2 7.9 %collective-permute-start = (f32[5,2,8,256]{3,2,1,0:T(8,128)S(1)}, f32[5,2,8,256]{3,2,1,0:T(8,128)S(1)}, u32[]{:S(2)}, u32[]{:S(2)}) collective-permute-start(f32[5,2,8,256]{3,2,1,0:T(8,128)S(1)} %get-tuple-element.43), channel_id=1, source_target_pairs={{0,1},{1,2},{2,3},{3,4},{4,5},{5,6},{6,7},{7,8},{8,9},{9,10},{10,1... | collective-permute-start | bytes 245768 | tf_op jit(solution)/shard_map/ppermute | solution.py:369
  4.2 4.9 %collective-permute-start.1 = (f32[5,2,8,256]{3,2,1,0:T(8,128)S(1)}, f32[5,2,8,256]{3,2,1,0:T(8,128)S(1)}, u32[]{:S(2)}, u32[]{:S(2)}) collective-permute-start(f32[5,2,8,256]{3,2,1,0:T(8,128)S(1)} %get-tuple-element.44), channel_id=1, source_target_pairs={{0,15},{1,0},{2,1},{3,2},{4,3},{5,4},{6,5},{7,6},{8,7},{9,8},{10,9... | collective-permute-start | bytes 245768 | tf_op jit(solution)/shard_map/ppermute | solution.py:380
  7.1 5.8 %collective-permute-start.2 = (f32[80,256]{1,0:T(8,128)S(1)}, f32[80,256]{1,0:T(8,128)S(1)}, u32[]{:S(2)}, u32[]{:S(2)}) collective-permute-start(f32[80,256]{1,0:T(8,128)S(1)} %get-tuple-element.47), channel_id=1, source_target_pairs={{0,16},{16,0},{1,17},{17,1},{2,18},{18,2},{3,19},{19,3},{4,20},{20... | collective-permute-start | bytes 245768 | tf_op jit(solution)/shard_map/ppermute | solution.py:391
  9.2 3.8 %collective-permute-start.3 = (f32[16,256]{1,0:T(8,128)S(1)}, f32[16,256]{1,0:T(8,128)S(1)}, u32[]{:S(2)}, u32[]{:S(2)}) collective-permute-start(f32[16,256]{1,0:T(8,128)S(1)} %get-tuple-element.48), channel_id=1, source_target_pairs={{0,16},{16,0},{1,17},{17,1},{2,18},{18,2},{3,19},{19,3},{4,20},{20... | collective-permute-start | bytes 49160 | tf_op jit(solution)/shard_map/ppermute | solution.py:415
